TPU v7x, 128 devices: a whole 4x4x4 slice. The times are simulated.
128 devices in a mesh: seq: 32 (over z_lo, y, x), dp: 4 (over z_hi, core).
Axes of the slice: x: 4, y: 4, z: 4 (z_hi: 2, z_lo: 2; z = z_hi * 2 + z_lo), core: 2. Of those that a mesh axis runs over, the one named last changes fastest.
Arguments:
- inputs: bfloat16 [4, 16384, 1024], P('dp', 'seq'), may hold values from -600 to 600
- cotangent: bfloat16 [4, 16384, 1024], P('dp', 'seq'), may hold values from -6 to 6
- gain: float32 [1024], replicated, may hold values from 0.5 to 1.5
- w_qkv: bfloat16 [1024, 3072], replicated, may hold values from -1.25 to 1.25
- w_out: bfloat16 [1024, 1024], replicated, may hold values from -0.1875 to 0.1875
- segment_ids: int32 [4, 16384], P('dp'), may hold values from 0 to 15, never falling along the last dimension, each value on 1 to 2048 neighbouring positions
Outputs:
- grad_inputs: bfloat16 [4, 16384, 1024], P('dp', 'seq')
- grad_qkv_weight: float32 [1024, 3072], P('seq')
Inputs may be any that keep to these rules, and one draw needn't show every extreme that they name: `segment_ids`: each row is non-decreasing; every document is 1 to 2048 bytes long and one is exactly 2048.
All inputs are finite; a program needn't handle non-finite values.
Results may differ from a plain program's by a relative error of at most 0.03.
Values may be sent and summed in bfloat16 or wider, within the bound.
A program may use at most 192 MiB of HBM per device.

v0:
```python
import jax
import jax.numpy as jnp
from jax import lax
from jax.sharding import PartitionSpec as P

HEADS = 16
WINDOW = 512


EPS = 1e-05


def from_behind(array, axis, by):
    peers = lax.axis_size(axis)
    pairs = [(i, i + by) for i in range(peers) if 0 <= i + by < peers]
    return lax.ppermute(array, axis, pairs)


def soft_probs(qblk, kblk, pos_q, pos_k, seg_q, seg_k, heads):
    qh = qblk.reshape(qblk.shape[0], heads, -1)
    kh = kblk.reshape(kblk.shape[0], heads, -1)
    scores = jnp.einsum("qhd,khd->hqk", qh, kh, preferred_element_type=jnp.float32) * qh.shape[
        2
    ] ** (-0.5)
    allowed = (
        (pos_k[None, :] <= pos_q[:, None])
        & (pos_q[:, None] - pos_k[None, :] < WINDOW)
        & (seg_k[None, :] == seg_q[:, None])
    )
    scores = jnp.where(allowed[None], scores, -1e30)
    top = jnp.max(scores, axis=2, keepdims=True)
    expo = jnp.exp(scores - top)
    return expo / jnp.sum(expo, axis=2, keepdims=True)


def body(inputs, cotangent, gain, w_qkv, w_out, segment_ids):
    x_rows = inputs[0]
    grad_out = cotangent[0]
    rows, width = x_rows.shape
    heads = HEADS
    scale = (width // heads) ** (-0.5)
    xf = x_rows.astype(jnp.float32)
    inv_rms = lax.rsqrt(jnp.mean(xf * xf, axis=1, keepdims=True) + EPS)
    normal_x = xf * inv_rms
    normed = (normal_x * gain).astype(jnp.bfloat16)
    qkv = jnp.dot(normed, w_qkv, preferred_element_type=jnp.float32).astype(jnp.bfloat16)
    queries = qkv[:, :width]
    before = from_behind(qkv[rows - WINDOW :, width:], "seq", 1)
    keys_ext = jnp.concatenate([before[:, :width], qkv[:, width : 2 * width]], 0)
    values_ext = jnp.concatenate([before[:, width:], qkv[:, 2 * width :]], 0)
    offset = lax.axis_index("seq") * rows
    seg_padded = jnp.concatenate([jnp.full((WINDOW,), -1, jnp.int32), segment_ids[0]], 0)
    seg_ext = lax.dynamic_slice_in_dim(seg_padded, offset, WINDOW + rows, 0)
    pos_ext = offset - WINDOW + jnp.arange(WINDOW + rows, dtype=jnp.int32)
    block = min(512, rows)
    span = WINDOW + block

    def block_probs(first):
        return soft_probs(
            queries,
            keys_ext,
            pos_ext[WINDOW + first : WINDOW + first + block],
            pos_ext,
            seg_ext[WINDOW + first : WINDOW + first + block],
            seg_ext,
            heads,
        )

    index = 0
    first = index * block
    probs = block_probs(first)
    value_heads = values_ext.reshape(span, heads, -1)
    out = jnp.einsum(
        "hqk,khd->qhd", probs.astype(jnp.bfloat16), value_heads, preferred_element_type=jnp.float32
    )
    outputs = out.astype(jnp.bfloat16).reshape(block, width)
    d_attn = lax.dot_general(
        grad_out, w_out, (((1,), (1,)), ((), ())), preferred_element_type=jnp.float32
    ).astype(jnp.bfloat16)
    grad_keys = jnp.zeros((WINDOW + rows, width), jnp.float32)
    grad_values = jnp.zeros((WINDOW + rows, width), jnp.float32)
    index = 0
    first = index * block
    probs = block_probs(first)
    probs_low = probs.astype(jnp.bfloat16)
    query_heads = queries.reshape(block, heads, -1)
    key_heads = keys_ext.reshape(span, heads, -1)
    value_heads = values_ext.reshape(span, heads, -1)
    grad_heads = d_attn.reshape(block, heads, -1)
    out_heads = outputs.reshape(block, heads, -1)
    delta = jnp.sum(grad_heads.astype(jnp.float32) * out_heads.astype(jnp.float32), axis=2)
    dprob = jnp.einsum("qhd,khd->hqk", grad_heads, value_heads, preferred_element_type=jnp.float32)
    dscore = (probs * (dprob - delta.T[:, :, None]) * scale).astype(jnp.bfloat16)
    grad_q = jnp.einsum("hqk,khd->qhd", dscore, key_heads, preferred_element_type=jnp.float32)
    grad_queries = grad_q.astype(jnp.bfloat16).reshape(block, width)
    part_k = jnp.einsum("hqk,qhd->khd", dscore, query_heads, preferred_element_type=jnp.float32)
    part_v = jnp.einsum("hqk,qhd->khd", probs_low, grad_heads, preferred_element_type=jnp.float32)
    grad_keys = grad_keys.at[first : first + span].add(part_k.reshape(span, width))
    grad_values = grad_values.at[first : first + span].add(part_v.reshape(span, width))
    grad_kv = jnp.concatenate([grad_keys, grad_values], 1)
    returned = from_behind(grad_kv[:WINDOW].astype(jnp.bfloat16), "seq", -1)
    own_kv = (
        grad_kv[WINDOW:].at[rows - WINDOW :].add(returned.astype(jnp.float32)).astype(jnp.bfloat16)
    )
    grad_qkv = jnp.concatenate([grad_queries, own_kv], 1)
    grad_normed = lax.dot_general(
        grad_qkv, w_qkv, (((1,), (1,)), ((), ())), preferred_element_type=jnp.float32
    )
    scaled = grad_normed * gain
    grad_x = (
        grad_out.astype(jnp.float32)
        + (scaled - normal_x * jnp.mean(scaled * normal_x, axis=1, keepdims=True)) * inv_rms
    )
    groups = lax.axis_size("dp")
    share = lax.psum_scatter(
        lax.dot_general(
            normed, grad_qkv, (((0,), (0,)), ((), ())), preferred_element_type=jnp.float32
        ).astype(jnp.bfloat16),
        "seq",
        scatter_dimension=0,
        tiled=True,
    )
    total = lax.psum(share, "dp").astype(jnp.float32)
    factor = 1.0 / groups
    return (grad_x.astype(jnp.bfloat16)[None], total * factor)


def solution(mesh):
    return jax.shard_map(
        body,
        mesh=mesh,
        in_specs=(P("dp", "seq", None), P("dp", "seq", None), P(), P(), P(), P("dp", None)),
        out_specs=(P("dp", "seq", None), P("seq", None)),
        check_vma=False,
    )
```

profile of v0, /device:TPU:1, one launch (start us, length us, event | category | flops | bytes accessed | tf_op | source)
XLA Modules:
  0.0 450.9 jit_solution(14268944761630230846)
XLA Ops:
  8.9 6.6 %convolution_convert_fusion.1 = bf16[512,3072]{1,0:T(8,128)(2,1)S(1)} fusion(bf16[1024,3072]{1,0:T(8,128)(2,1)} %param.21, bf16[1,512,1024]{2,1,0:T(8,128)(2,1)} %param.18, f32[1024]{0:T(1024)} %param.20, f32[512]{0:T(512)S(1)} %add_rsqrt_fusion), kind=kOutput, calls=%fused_computation.13 | convolution fusion | flops 3224895488 | bytes 10491904 | tf_op jit(solution)/shard_map/dot_general | solution.py:46
  18.7 5.4 %collective-permute-start = (bf16[512,2048]{1,0:T(8,128)(2,1)}, bf16[512,2048]{1,0:T(8,128)(2,1)}, u32[]{:S(2)}, u32[]{:S(2)}) collective-permute-start(bf16[512,2048]{1,0:T(8,128)(2,1)} %slice.85), channel_id=1, source_target_pairs={{0,4},{4,8},{8,12},{12,16},{16,20},{20,24},{24,28},{28,32},{32,36}... | collective-permute-start | bytes 6291464 | tf_op jit(solution)/shard_map/ppermute | solution.py:16
  24.3 2.3 convolution_convert_fusion.4
  28.0 3.5 fusion.34
  32.8 34.4 %collective-permute-done = bf16[512,2048]{1,0:T(8,128)(2,1)} collective-permute-done((bf16[512,2048]{1,0:T(8,128)(2,1)}, bf16[512,2048]{1,0:T(8,128)(2,1)}, u32[]{:S(2)}, u32[]{:S(2)}) %collective-permute-start) | collective-permute-done | bytes 2097184 | tf_op jit(solution)/shard_map/ppermute | solution.py:16
  67.2 1.7 fusion.35
  69.0 2.4 pad_maximum_fusion.2
  71.4 3.9 copy.17
  75.3 3.9 copy.20
  79.2 18.7 %fusion.36 = (f32[16,512]{1,0:T(8,128)S(1)}, f32[16,512,1024]{2,1,0:T(8,128)}) fusion(pred[512,1024]{1,0:T(8,128)(4,1)S(1)} %fusion.22, bf16[512,16,64]{0,2,1:T(8,128)(2,1)S(1)} %bitcast.61, bf16[1024,16,64]{0,2,1:T(8,128)(2,1)} %bitcast.57), kind=kOutput, calls=%fused_computation.57 | convolution fusion | flops 1107297280 | bytes 37257216 | tf_op jit(solution)/shard_map/sub | solution.py:32
  97.9 13.1 %fusion.5 = bf16[16,512,1024]{2,1,0:T(8,128)(2,1)S(1)} fusion(f32[16,512,1024]{2,1,0:T(8,128)} %get-tuple-element.68, f32[16,512]{1,0:T(8,128)S(1)} %get-tuple-element.67), kind=kLoop, calls=%fused_computation.9 | loop fusion | flops 16777216 | bytes 50364416 | tf_op jit(solution)/shard_map/convert_element_type | solution.py:74
  111.0 5.8 %fusion.38 = f32[16,64,1024]{2,1,0:T(8,128)} fusion(bf16[512,16,64]{0,2,1:T(8,128)(2,1)S(1)} %bitcast.54, bf16[16,512,1024]{2,1,0:T(8,128)(2,1)S(1)} %fusion.5), kind=kOutput, calls=%fused_computation.59 | convolution fusion | flops 1073741824 | bytes 22020096 | tf_op jit(solution)/shard_map/hqk,qhd->khd/dot_general | solution.py:97
  118.0 11.6 %fusion.20 = f32[512,16]{0,1:T(8,128)S(1)} fusion(bf16[512,16,64]{0,2,1:T(8,128)(2,1)S(1)} %bitcast.55, bf16[1024,16,64]{0,2,1:T(8,128)(2,1)} %bitcast.59, bf16[16,512,1024]{2,1,0:T(8,128)(2,1)} %copy-done.2), kind=kOutput, calls=%fused_computation.35 | convolution fusion | flops 1076355072 | bytes 19955712 | tf_op jit(solution)/shard_map/hqk,khd->qhd/dot_general | solution.py:73
  129.6 18.6 %multiply_convert_fusion = bf16[16,512,1024]{2,1,0:T(8,128)(2,1)} fusion(f32[16,512]{1,0:T(8,128)S(1)} %bitcast.66, f32[16,512,1024]{2,1,0:T(8,128)} %get-tuple-element.68, f32[16,512]{1,0:T(8,128)S(1)} %get-tuple-element.67, bf16[512,16,64]{0,2,1:T(8,128)(2,1)S(1)} %bitcast.56, bf16[1024,16,64]{0,2,1:T(8,128)(2,1)} %bitcast.60), kind=kOutput, calls=%fused_computation.1 | convolution fusion | flops 1115684864 | bytes 53542912 | tf_op jit(solution)/shard_map/qhd,khd->hqk/dot_general | solution.py:92
  148.2 8.9 %fusion.37 = f32[16,64,1024]{2,1,0:T(8,128)S(1)} fusion(bf16[512,16,64]{0,2,1:T(8,128)(2,1)S(1)} %bitcast.62, bf16[16,512,1024]{2,1,0:T(8,128)(2,1)} %multiply_convert_fusion), kind=kOutput, calls=%fused_computation.58 | convolution fusion | flops 1073741824 | bytes 22020096 | tf_op jit(solution)/shard_map/hqk,qhd->khd/dot_general | solution.py:96
  161.5 11.9 %convolution_convert_fusion.2 = bf16[16,64,512]{2,1,0:T(8,128)(2,1)} fusion(bf16[1024,16,64]{0,2,1:T(8,128)(2,1)S(1)} %bitcast.58, bf16[16,512,1024]{2,1,0:T(8,128)(2,1)} %multiply_convert_fusion), kind=kOutput, calls=%fused_computation.40 | convolution fusion | flops 1074266112 | bytes 19922944 | tf_op jit(solution)/shard_map/hqk,khd->qhd/dot_general | solution.py:94
  173.5 35.3 %collective-permute-done.1 = bf16[512,2048]{0,1:T(8,128)(2,1)} collective-permute-done((bf16[512,2048]{0,1:T(8,128)(2,1)}, bf16[512,2048]{0,1:T(8,128)(2,1)}, u32[]{:S(2)}, u32[]{:S(2)}) %collective-permute-start.1) | collective-permute-done | bytes 2097184 | tf_op jit(solution)/shard_map/ppermute | solution.py:16
  208.8 3.6 fusion.8
  212.4 6.8 %convolution_convert_fusion = bf16[1024,3072]{1,0:T(8,128)(2,1)} fusion(bf16[512,2048]{0,1:T(8,128)(2,1)S(1)} %fusion.8, bf16[512,1024]{0,1:T(8,128)(2,1)S(1)} %bitcast.64, bf16[1,512,1024]{2,1,0:T(8,128)(2,1)S(1)} %copy-done.7, f32[1024]{0:T(1024)S(1)} %copy-done.14, f32[512]{0:T(512)S(1)} %add_rsqrt_fusion), kind=kOutput, calls=%fused_computation.12 | convolution fusion | flops 3232759808 | bytes 10491904 | tf_op jit(solution)/shard_map/dot_general | solution.py:116
  219.3 8.9 %fusion.14 = (f32[512]{0:T(512)S(1)}, f32[512,1024]{1,0:T(8,128)}) fusion(bf16[1,512,1024]{2,1,0:T(8,128)(2,1)S(1)} %copy-done.7, f32[1024]{0:T(1024)S(1)} %copy-done.14, f32[512]{0:T(512)S(1)} %add_rsqrt_fusion, bf16[1024,3072]{1,0:T(8,128)(2,1)} %param.21, bf16[512,2048]{0,1:T(8,128)(2,1)} %copy-done.10, bf16[512,1024]{0,1:T(8,128)(2,1)} %bitcast.63), kind=kOutput, calls=%fused_computation.26 | convolution fusion | flops 3230137856 | bytes 12591104 | tf_op jit(solution)/shard_map/dot_general | solution.py:106
  228.2 151.2 %reduce-scatter.2.cloned.1.call-done = bf16[32,3072]{1,0:T(8,128)(2,1)} async-done(((bf16[1024,3072]{1,0:T(8,128)(2,1)}), bf16[32,3072]{1,0:T(8,128)(2,1)}) %reduce-scatter.2.cloned.1.call-update) | async-done | bytes 196624 | tf_op jit(solution)/shard_map/reduce_scatter | solution.py:115
  379.4 3.5 fusion.24
  382.9 59.1 %all-reduce.3.cloned.1.call-done = bf16[32,3072]{1,0:T(8,128)(2,1)} async-done(((bf16[32,3072]{1,0:T(8,128)(2,1)}), bf16[32,3072]{1,0:T(8,128)(2,1)}) %all-reduce.3.cloned.1.call-update) | async-done | bytes 196624 | tf_op jit(solution)/shard_map/psum | solution.py:123
  442.0 1.7 convert_multiply_fusion.2
  (46 shorter events, 13.3 us)
Async XLA Ops:
  7.2 17.1 %copy-start = (bf16[1024,1024]{1,0:T(8,128)(2,1)S(1)}, bf16[1024,1024]{1,0:T(8,128)(2,1)}, u32[]{:S(2)}) copy-start(bf16[1024,1024]{1,0:T(8,128)(2,1)} %param.22) | copy-start | bytes 6291460
  7.2 372.2 %reduce-scatter.2.cloned.1.call-start = ((), (), s32[]{:S(2)}) async-start(), calls=%async_computation.1 | async-start | bytes 6488064 | tf_op jit(solution)/shard_map/reduce_scatter | solution.py:115
  15.5 1.6 copy-start.5
  17.2 7.0 %copy-start.13 = (s32[1,16384]{1,0:T(1,128)S(1)}, s32[1,16384]{1,0:T(1,128)}, u32[]{:S(2)}) copy-start(s32[1,16384]{1,0:T(1,128)} %param.23) | copy-start | bytes 196612
  17.2 7.1 %copy-start.11 = (bf16[1,512,1024]{2,1,0:T(8,128)(2,1)S(1)}, bf16[1,512,1024]{2,1,0:T(8,128)(2,1)}, u32[]{:S(2)}) copy-start(bf16[1,512,1024]{2,1,0:T(8,128)(2,1)} %param.19) | copy-start | bytes 3145732
  18.7 48.5 %collective-permute-start = (bf16[512,2048]{1,0:T(8,128)(2,1)}, bf16[512,2048]{1,0:T(8,128)(2,1)}, u32[]{:S(2)}, u32[]{:S(2)}) collective-permute-start(bf16[512,2048]{1,0:T(8,128)(2,1)} %slice.85), channel_id=1, source_target_pairs={{0,4},{4,8},{8,12},{12,16},{16,20},{20,24},{24,28},{28,32},{32,36}... | collective-permute-start | bytes 6291464 | tf_op jit(solution)/shard_map/ppermute | solution.py:16
  32.1 36.8 %copy-start.8 = (bf16[512,1024]{1,0:T(8,128)(2,1)S(1)}, bf16[512,1024]{1,0:T(8,128)(2,1)}, u32[]{:S(2)}) copy-start(bf16[512,1024]{1,0:T(8,128)(2,1)} %get-tuple-element.62) | copy-start | bytes 3145732
  32.1 36.8 %copy-start.9 = (bf16[512,1024]{1,0:T(8,128)(2,1)S(1)}, bf16[512,1024]{1,0:T(8,128)(2,1)}, u32[]{:S(2)}) copy-start(bf16[512,1024]{1,0:T(8,128)(2,1)} %get-tuple-element.63) | copy-start | bytes 3145732
  111.0 7.0 %copy-start.2 = (bf16[16,512,1024]{2,1,0:T(8,128)(2,1)}, bf16[16,512,1024]{2,1,0:T(8,128)(2,1)S(1)}, u32[]{:S(2)}) copy-start(bf16[16,512,1024]{2,1,0:T(8,128)(2,1)S(1)} %fusion.5) | copy-start | bytes 50331652
  148.2 9.0 %copy-start.3 = (f32[16,64,1024]{2,1,0:T(8,128)S(1)}, f32[16,64,1024]{2,1,0:T(8,128)}, u32[]{:S(2)}) copy-start(f32[16,64,1024]{2,1,0:T(8,128)} %fusion.38) | copy-start | bytes 12582916
  157.2 2.8 copy-start.4
  157.2 4.3 copy-start.6
  160.0 48.8 %collective-permute-start.1 = (bf16[512,2048]{0,1:T(8,128)(2,1)}, bf16[512,2048]{0,1:T(8,128)(2,1)}, u32[]{:S(2)}, u32[]{:S(2)}) collective-permute-start(bf16[512,2048]{0,1:T(8,128)(2,1)} %fusion.9), channel_id=1, source_target_pairs={{4,0},{8,4},{12,8},{16,12},{20,16},{24,20},{28,24},{32,28},{36,32}... | collective-permute-start | bytes 6291464 | tf_op jit(solution)/shard_map/ppermute | solution.py:16
  173.5 38.9 %copy-start.7 = (bf16[1,512,1024]{2,1,0:T(8,128)(2,1)S(1)}, bf16[1,512,1024]{2,1,0:T(8,128)(2,1)}, u32[]{:S(2)}) copy-start(bf16[1,512,1024]{2,1,0:T(8,128)(2,1)} %param.18) | copy-start | bytes 3145732
  173.5 38.9 %copy-start.12 = (bf16[16,64,512]{2,1,0:T(8,128)(2,1)S(1)}, bf16[16,64,512]{2,1,0:T(8,128)(2,1)}, u32[]{:S(2)}) copy-start(bf16[16,64,512]{2,1,0:T(8,128)(2,1)} %convolution_convert_fusion.2) | copy-start | bytes 3145732
  173.5 38.9 %copy-start.14 = (f32[1024]{0:T(1024)S(1)}, f32[1024]{0:T(1024)}, u32[]{:S(2)}) copy-start(f32[1024]{0:T(1024)} %param.20) | copy-start | bytes 12292
  212.3 6.9 %copy-start.10 = (bf16[512,2048]{0,1:T(8,128)(2,1)}, bf16[512,2048]{0,1:T(8,128)(2,1)S(1)}, u32[]{:S(2)}) copy-start(bf16[512,2048]{0,1:T(8,128)(2,1)S(1)} %fusion.8) | copy-start | bytes 6291460
  219.2 222.7 %all-reduce.3.cloned.1.call-start = ((), (), s32[]{:S(2)}) async-start(), calls=%async_computation.2 | async-start | bytes 393216 | tf_op jit(solution)/shard_map/psum | solution.py:123
  219.3 224.4 %copy-start.1 = (bf16[1024,1024]{1,0:T(8,128)(2,1)S(1)}, bf16[1024,1024]{1,0:T(8,128)(2,1)}, u32[]{:S(2)}) copy-start(bf16[1024,1024]{1,0:T(8,128)(2,1)} %param.22) | copy-start | bytes 6291460
Sparse Core Ops, SparseCore 0:
  219.3 160.0 reduce-scatter.1
  381.9 60.0 all-reduce.2
where the time goes:
time: 454 us; the launch traced here: 451 us
  waiting for transfers between devices  280 us (62%)
  matrix products  100 us (22%)
  other arithmetic  28.3 us (6%)
  local copies, waits for them, and re-layouts  20.7 us (5%)
  between operations  14.7 us (3%)
  starting transfers between devices  7.05 us (2%)
    reduce_scatter x1, waiting for transfers between devices, body(): lax.psum_scatter(lax.dot_general(normed, grad_qkv, (((0,), (0,)), ((), ()...  151 us
    ppermute x2, waiting for transfers between devices, from_behind(): return lax.ppermute(array, axis, pairs)  69.7 us
    psum x1, waiting for transfers between devices, body(): total = lax.psum(share, 'dp').astype(jnp.float32)  59.1 us
    sub x1, matrix products, soft_probs(): expo = jnp.exp(scores - top)  18.7 us
    dot_general x1, matrix products, body(): jnp.einsum('qhd,khd->hqk', grad_heads, value_heads, preferred_element_typ...  18.6 us
    convert_element_type x1, other arithmetic, body(): probs.astype(jnp.bfloat16)  13.1 us
    dot_general x1, matrix products, body(): jnp.einsum('hqk,khd->qhd', dscore, key_heads, preferred_element_type=jnp....  11.9 us
    dot_general x1, matrix products, body(): jnp.einsum('hqk,khd->qhd', probs.astype(jnp.bfloat16), value_heads, prefe...  11.6 us
  transfers between devices with their start and end apart: 4, of which 4 were waited for; matrix products, arithmetic and copies ran while one was open for 7% of the time, Pallas kernels for 0%

commit v1 on v0

v1 whole, which is shorter than its diff:
```python
import functools
import math

import jax
import jax.numpy as jnp
from jax import lax
from jax.experimental import pallas as pl
from jax.experimental.pallas import tpu as pltpu
from jax.sharding import PartitionSpec as P

MESH = pl.DeviceIdType.MESH
F32 = jnp.float32
BF16 = jnp.bfloat16

WINDOW = 512
ROWS = 512
EXT = WINDOW + ROWS
D = 1024
PAIR = 128
PAIRS = D // PAIR
QB = 128
NQ = ROWS // QB
SPAN = WINDOW + QB
TILE = 256
HALF = 256
CHUNKS = 6
EPS = 1e-05
SCALE = 0.125
LOG2E = math.log2(math.e)

NT = (((1,), (1,)), ((), ()))

ORDERS = (
    ("yw", "zu", "yu", "zw", "xw", "xu"),
    ("zw", "yu", "zu", "yw", "xu", "xw"),
    ("yu", "zw", "yw", "zu", "xw", "xu"),
    ("zu", "yw", "zw", "yu", "xu", "xw"),
    ("yw", "zw", "yu", "zu", "xw", "xu"),
    ("zw", "yw", "zu", "yu", "xu", "xw"),
)
STEPS = len(ORDERS[0])
BLOCK = 16
BLOCKS = D // BLOCK


def gray(place):
    return {"u": place // 2, "w": (place // 2 + place) % 2}


def block_places(order):
    places = []
    for block in range(BLOCKS):
        zh, seq = block % 2, block // 2
        at = {"x": seq % 4, "y": seq // 4 % 4, "z": zh * 2 + seq // 16}
        place = 0
        for bit in order:
            place = place * 2 + gray(at[bit[0]])[bit[1]]
        places.append(place)
    return places


def kernel(
    x_hbm,
    cot_hbm,
    gain_ref,
    w_hbm,
    wo_hbm,
    segq_ref,
    segk_ref,
    gx_ref,
    gw_ref,
    x_ref,
    cot_ref,
    w_ref,
    wo_ref,
    xh_ref,
    normed_ref,
    nt_ref,
    q_ref,
    k_ref,
    v_ref,
    kt_ref,
    do_ref,
    mask_ref,
    dq_ref,
    dk_ref,
    dv_ref,
    acck_ref,
    accv_ref,
    back_send,
    back_recv,
    gn_ref,
    own_ref,
    sib_send,
    sib_recv,
    rs_recv,
    gather_ref,
    load_sem,
    halo_sem,
    back_sem,
    sib_sem,
    rs_send_sem,
    rs_recv_sem,
    gather_sem,
):
    s = lax.axis_index("seq")
    d = lax.axis_index("dp")
    x, y, zl = s % 4, s // 4 % 4, s // 16
    core, zh = d % 2, d // 2
    z = zh * 2 + zl

    def device(x, y, z, core):
        return {"seq": z % 2 * 16 + y * 4 + x, "dp": z // 2 * 2 + core}

    nxt = {"seq": (s + 1) % 32, "dp": d}
    prev = {"seq": (s + 31) % 32, "dp": d}

    def flip(place, bit):
        return 3 - place if bit == "u" else place + 1 - 2 * (place % 2)

    partners = {}
    mine = {}
    for axis, place in (("x", x), ("y", y), ("z", z)):
        for bit in "uw":
            at = {"x": x, "y": y, "z": z, axis: flip(place, bit)}
            partners[axis + bit] = device(at["x"], at["y"], at["z"], core)
            mine[axis + bit] = gray(place)[bit]
    sibling = {"seq": s, "dp": zh * 2 + 1 - core}
    others = [
        {"seq": s, "dp": zh * 2 + 1 - core},
        {"seq": s, "dp": (1 - zh) * 2 + core},
        {"seq": s, "dp": (1 - zh) * 2 + 1 - core},
    ]

    loads = []
    for index, (src, dst) in enumerate(
        ((x_hbm, x_ref), (cot_hbm, cot_ref), (wo_hbm, wo_ref), (w_hbm, w_ref))
    ):
        loads.append(pltpu.make_async_copy(src, dst, load_sem.at[index]))
        loads[-1].start()

    barrier = pltpu.get_barrier_semaphore()
    peers = [nxt, prev, *partners.values(), *others]
    for peer in peers:
        pl.semaphore_signal(barrier, inc=1, device_id=peer, device_id_type=MESH)
    pl.semaphore_wait(barrier, len(peers))

    halos = []
    for piece in range(NQ):
        rows = pl.ds(piece * QB, QB)
        halos.append(
            pltpu.make_async_remote_copy(
                src_ref=x_hbm.at[rows],
                dst_ref=xh_ref.at[rows],
                send_sem=halo_sem.at[0, piece],
                recv_sem=halo_sem.at[1, piece],
                device_id=nxt,
                device_id_type=MESH,
            )
        )
    for piece in reversed(range(NQ)):
        halos[piece].start()

    gain = gain_ref[...]

    def norm_rows(src_ref, row, ext_row):
        xf = src_ref[pl.ds(row, QB), :].astype(F32)
        inv = lax.rsqrt(jnp.mean(xf * xf, axis=1, keepdims=True) + EPS)
        normed = (xf * inv * gain).astype(BF16)
        normed_ref[pl.ds(ext_row, QB), :] = normed
        return normed

    loads[0].wait()

    for j in range(NQ):
        normed = norm_rows(x_ref, j * QB, WINDOW + j * QB)
        nt_ref[:, WINDOW + j * QB : WINDOW + (j + 1) * QB] = normed.T

    lane = lax.broadcasted_iota(jnp.int32, (SPAN, QB), 1)
    row = lax.broadcasted_iota(jnp.int32, (SPAN, QB), 0)
    in_window = (row > lane) & (row <= lane + WINDOW)
    for j in range(NQ):
        same = segk_ref[j * QB : j * QB + SPAN, :] == segq_ref[:, j * QB : (j + 1) * QB]
        mask_ref[j] = jnp.where(in_window & same, 0.0, -1e30).astype(F32)

    loads[1].wait()
    loads[2].wait()

    @pl.loop(0, D // TILE)
    def _(n):
        at = pl.ds(pl.multiple_of(n * TILE, TILE), TILE)
        do_ref[:, at] = lax.dot_general(
            cot_ref[...], wo_ref[at, :], NT, preferred_element_type=F32
        ).astype(BF16)

    loads[3].wait()

    def keys_values(first, count):
        @pl.loop(0, D // TILE)
        def _(n):
            at = pl.ds(pl.multiple_of(n * TILE, TILE), TILE)
            at_k = pl.ds(pl.multiple_of(D + n * TILE, TILE), TILE)
            at_v = pl.ds(pl.multiple_of(2 * D + n * TILE, TILE), TILE)
            normed = normed_ref[first : first + count, :]
            k = jnp.dot(normed, w_ref[:, at_k], preferred_element_type=F32).astype(BF16)
            k_ref[first : first + count, at] = k
            kt_ref[at, first : first + count] = k.T
            v = jnp.dot(normed, w_ref[:, at_v], preferred_element_type=F32).astype(BF16)
            v_ref[first : first + count, at] = v

    @pl.loop(0, D // TILE)
    def _(n):
        at = pl.ds(pl.multiple_of(n * TILE, TILE), TILE)
        q_ref[:, at] = jnp.dot(
            normed_ref[WINDOW:, :], w_ref[:, at], preferred_element_type=F32
        ).astype(BF16)

    keys_values(WINDOW, ROWS)

    first_head = lax.broadcasted_iota(jnp.int32, (QB, PAIR), 1) < PAIR // 2
    zero = jnp.zeros((QB, PAIR), BF16)

    def two_heads(block):
        return jnp.concatenate(
            [jnp.where(first_head, block, zero), jnp.where(first_head, zero, block)], 0
        )

    def attend(j, pair):
        at = pl.ds(pl.multiple_of(pair * PAIR, PAIR), PAIR)
        lo = j * QB
        queries = two_heads(q_ref[lo : lo + QB, at])
        grads = two_heads(do_ref[lo : lo + QB, at])
        scores = lax.dot_general(
            k_ref[lo : lo + SPAN, at], queries, NT, preferred_element_type=F32
        )
        dprob = lax.dot_general(
            v_ref[lo : lo + SPAN, at], grads, NT, preferred_element_type=F32
        )
        mask = mask_ref[j]
        scores = scores * (SCALE * LOG2E) + jnp.concatenate([mask, mask], 1)
        expo = jnp.exp2(scores - jnp.max(scores, axis=0, keepdims=True))
        inverse = 1.0 / jnp.sum(expo, axis=0, keepdims=True)
        probs = expo * inverse
        delta = jnp.sum(probs * dprob, axis=0, keepdims=True)
        dscore = (probs * (dprob - delta)).astype(BF16)
        part_v = jnp.dot(probs.astype(BF16), grads, preferred_element_type=F32)
        part_k = jnp.dot(dscore, queries, preferred_element_type=F32)
        dq_t = jnp.dot(kt_ref[at, lo : lo + SPAN], dscore, preferred_element_type=F32)
        dq_t = jnp.concatenate(
            [dq_t[: PAIR // 2, :QB], dq_t[PAIR // 2 :, QB:]], 0
        )
        dq_ref[lo : lo + QB, at] = (dq_t.T * SCALE).astype(BF16)
        fresh = SPAN if j == NQ - 1 else QB
        done = SPAN if j == 0 else QB
        for part, acc_ref, out_ref, scale in (
            (part_v, accv_ref, dv_ref, 1.0),
            (part_k, acck_ref, dk_ref, SCALE),
        ):
            for r in range(0, SPAN, QB):
                value = part[r : r + QB]
                if r >= fresh:
                    value = acc_ref[lo + r : lo + r + QB, at] + value
                if r >= SPAN - done:
                    out_ref[lo + r : lo + r + QB, at] = (value * scale).astype(BF16)
                else:
                    acc_ref[lo + r : lo + r + QB, at] = value

    for j in reversed(range(NQ)):
        halos[j].wait_recv()
        normed = norm_rows(xh_ref, j * QB, j * QB)
        nt_ref[:, j * QB : (j + 1) * QB] = normed.T
        keys_values(j * QB, QB)

        @pl.loop(0, PAIRS // 2)
        def _(p):
            attend(j, p * 2)
            attend(j, p * 2 + 1)

    backs = []
    for n in range(D // TILE):
        at = pl.ds(n * TILE, TILE)
        back_send[n] = (
            lax.dot_general(
                dk_ref[:WINDOW, :], w_ref[at, D : 2 * D], NT, preferred_element_type=F32
            )
            + lax.dot_general(
                dv_ref[:WINDOW, :], w_ref[at, 2 * D :], NT, preferred_element_type=F32
            )
        ).astype(BF16)
        copy = pltpu.make_async_remote_copy(
            src_ref=back_send.at[n],
            dst_ref=back_recv.at[n],
            send_sem=back_sem.at[0, n],
            recv_sem=back_sem.at[1, n],
            device_id=prev,
            device_id_type=MESH,
        )
        copy.start()
        backs.append(copy)

    places = [block_places(order) for order in ORDERS]

    def weight_half(c, half, out_ref):
        part, lo = c // 2, c % 2 * 2 * HALF
        at = pl.ds(pl.multiple_of(lo + half * HALF, HALF), HALF)
        if part == 0:
            value = jnp.dot(
                nt_ref[:, WINDOW:], dq_ref[:, at], preferred_element_type=F32
            )
        else:
            grads = dk_ref if part == 1 else dv_ref
            value = jnp.dot(nt_ref[...], grads[:, at], preferred_element_type=F32)
        value = value.astype(BF16)
        for block, place in enumerate(places[c]):
            out_ref[c, place * BLOCK : (place + 1) * BLOCK, :] = value[
                block * BLOCK : (block + 1) * BLOCK
            ]

    sends = []

    def sibling_copy(c):
        return pltpu.make_async_remote_copy(
            src_ref=sib_send.at[c],
            dst_ref=sib_recv.at[c],
            send_sem=sib_sem.at[0, c],
            recv_sem=sib_sem.at[1, c],
            device_id=sibling,
            device_id_type=MESH,
        )

    def base_of(c, t):
        base = 0
        for i in range(t):
            base = base + mine[ORDERS[c][i]] * (D >> (i + 1))
        return base

    def landing(t):
        return D - (D >> t)

    def halving_copy(c, t):
        length = D >> (t + 1)
        bit = ORDERS[c][t]
        away = pl.multiple_of(base_of(c, t) + (1 - mine[bit]) * length, BLOCK)
        return pltpu.make_async_remote_copy(
            src_ref=own_ref.at[c, pl.ds(away, length)],
            dst_ref=rs_recv.at[c, pl.ds(landing(t), length)],
            send_sem=rs_send_sem.at[c, t],
            recv_sem=rs_recv_sem.at[c, t],
            device_id=partners[bit],
            device_id_type=MESH,
        )

    halvings = {}
    sib_copies = {}

    def add_rows(c, first, src_ref, src_first, length):
        step = min(length, 128)

        @pl.loop(0, length // step)
        def _(i):
            to = pl.ds(pl.multiple_of(first + i * step, BLOCK), step)
            frm = pl.ds(pl.multiple_of(src_first + i * step, BLOCK), step)
            own_ref[c, to, :] = (
                own_ref[c, to, :].astype(F32) + src_ref[c, frm, :].astype(F32)
            ).astype(BF16)

    def stage(c, i):
        if i == 0:
            weight_half(c, 1 - core, sib_send)
            sib_copies[c] = sibling_copy(c)
            sib_copies[c].start()
            weight_half(c, core, own_ref)
        elif i == 1:
            sib_copies[c].wait_recv()
            add_rows(c, 0, sib_recv, 0, D)
            halvings[c, 0] = halving_copy(c, 0)
            halvings[c, 0].start()
        else:
            t = i - 2
            halvings[c, t].wait_recv()
            add_rows(c, base_of(c, t + 1), rs_recv, landing(t), D >> (t + 1))
            if t + 1 < STEPS:
                halvings[c, t + 1] = halving_copy(c, t + 1)
                halvings[c, t + 1].start()

    def own_grad(n):
        at = pl.ds(n * TILE, TILE)
        gn_ref[:, n * TILE : (n + 1) * TILE] = (
            lax.dot_general(dq_ref[...], w_ref[at, :D], NT, preferred_element_type=F32)
            + lax.dot_general(
                dk_ref[WINDOW:, :], w_ref[at, D : 2 * D], NT, preferred_element_type=F32
            )
            + lax.dot_general(
                dv_ref[WINDOW:, :], w_ref[at, 2 * D :], NT, preferred_element_type=F32
            )
        )

    def grad_rows(j):
        rows = slice(j * QB, (j + 1) * QB)
        back = jnp.concatenate([back_recv[n, rows, :] for n in range(D // TILE)], 1)
        xf = x_ref[rows, :].astype(F32)
        inv = lax.rsqrt(jnp.mean(xf * xf, axis=1, keepdims=True) + EPS)
        normal = xf * inv
        scaled = (gn_ref[rows, :] + back.astype(F32)) * gain
        grad = (
            cot_ref[rows, :].astype(F32)
            + (scaled - normal * jnp.mean(scaled * normal, axis=1, keepdims=True)) * inv
        )
        gx_ref[rows, :] = grad.astype(BF16)

    stages = STEPS + 2
    for tick in range(CHUNKS + stages - 1):
        for c in range(CHUNKS):
            if 0 <= tick - c < stages:
                stage(c, tick - c)
        if CHUNKS <= tick < CHUNKS + D // TILE:
            own_grad(tick - CHUNKS)
        if tick == CHUNKS + D // TILE:
            for copy in backs:
                copy.wait_recv()
        if CHUNKS + D // TILE <= tick:
            for j in (2 * (tick - CHUNKS - D // TILE), 2 * (tick - CHUNKS - D // TILE) + 1):
                if j < NQ:
                    grad_rows(j)

    for c in range(CHUNKS):
        rows = pl.ds(pl.multiple_of(base_of(c, STEPS), BLOCK), BLOCK)
        gather_ref[0, :, c * HALF : (c + 1) * HALF] = own_ref[c, rows, :]
    copies = []
    for i, other in enumerate(others):
        copy = pltpu.make_async_remote_copy(
            src_ref=gather_ref.at[0],
            dst_ref=gather_ref.at[i + 1],
            send_sem=gather_sem.at[0, i],
            recv_sem=gather_sem.at[1, i],
            device_id=other,
            device_id_type=MESH,
        )
        copy.start()
        copies.append(copy)
    for i in range(4):
        if i:
            copies[i - 1].wait_recv()
        from_zh = zh if i < 2 else 1 - zh
        from_core = core if i % 2 == 0 else 1 - core
        rows = pl.ds(pl.multiple_of(from_zh * BLOCK, BLOCK), BLOCK)
        for c in range(CHUNKS):
            at = pl.ds(pl.multiple_of(c * 2 * HALF + from_core * HALF, HALF), HALF)
            gw_ref[rows, at] = gather_ref[i, :, c * HALF : (c + 1) * HALF].astype(F32) * 0.25

    for copy in (*halos, *backs, *sib_copies.values(), *halvings.values(), *copies):
        copy.wait_send()


def body(inputs, cotangent, gain, w_qkv, w_out, segment_ids):
    offset = lax.axis_index("seq") * ROWS
    padded = jnp.concatenate([jnp.full((WINDOW,), -1, jnp.int32), segment_ids[0]], 0)
    seg = lax.dynamic_slice_in_dim(padded, offset, EXT, 0)
    any_space = pl.BlockSpec(memory_space=pl.ANY)
    vmem = pl.BlockSpec(memory_space=pltpu.VMEM)
    dma = pltpu.SemaphoreType.DMA
    grad_x, grad_w = pl.pallas_call(
        kernel,
        out_shape=(
            jax.ShapeDtypeStruct((ROWS, D), BF16),
            jax.ShapeDtypeStruct((2 * BLOCK, 3 * D), F32),
        ),
        in_specs=[any_space, any_space, vmem, any_space, any_space, vmem, vmem],
        out_specs=(vmem, vmem),
        scratch_shapes=[
            pltpu.VMEM((ROWS, D), BF16),
            pltpu.VMEM((ROWS, D), BF16),
            pltpu.VMEM((D, 3 * D), BF16),
            pltpu.VMEM((D, D), BF16),
            pltpu.VMEM((WINDOW, D), BF16),
            pltpu.VMEM((EXT, D), BF16),
            pltpu.VMEM((D, EXT), BF16),
            pltpu.VMEM((ROWS, D), BF16),
            pltpu.VMEM((EXT, D), BF16),
            pltpu.VMEM((EXT, D), BF16),
            pltpu.VMEM((D, EXT), BF16),
            pltpu.VMEM((ROWS, D), BF16),
            pltpu.VMEM((NQ, SPAN, QB), F32),
            pltpu.VMEM((ROWS, D), BF16),
            pltpu.VMEM((EXT, D), BF16),
            pltpu.VMEM((EXT, D), BF16),
            pltpu.VMEM((EXT, D), F32),
            pltpu.VMEM((EXT, D), F32),
            pltpu.VMEM((D // TILE, WINDOW, TILE), BF16),
            pltpu.VMEM((D // TILE, WINDOW, TILE), BF16),
            pltpu.VMEM((ROWS, D), F32),
            pltpu.VMEM((CHUNKS, D, HALF), BF16),
            pltpu.VMEM((CHUNKS, D, HALF), BF16),
            pltpu.VMEM((CHUNKS, D, HALF), BF16),
            pltpu.VMEM((CHUNKS, D, HALF), BF16),
            pltpu.VMEM((4, BLOCK, CHUNKS * HALF), BF16),
            dma((4,)),
            dma((2, NQ)),
            dma((2, D // TILE)),
            dma((2, CHUNKS)),
            dma((CHUNKS, STEPS)),
            dma((CHUNKS, STEPS)),
            dma((2, 3)),
        ],
        compiler_params=pltpu.CompilerParams(
            collective_id=0, has_side_effects=True, vmem_limit_bytes=60 * 1024 * 1024
        ),
    )(
        inputs[0],
        cotangent[0],
        gain[None],
        w_qkv,
        w_out,
        seg[None, WINDOW:],
        seg[:, None],
    )
    return grad_x[None], grad_w


def solution(mesh):
    return jax.shard_map(
        body,
        mesh=mesh,
        in_specs=(P("dp", "seq", None), P("dp", "seq", None), P(), P(), P(), P("dp", None)),
        out_specs=(P("dp", "seq", None), P("seq", None)),
        check_vma=False,
    )
```

time: 454 us -> 155 us (0.34)
  waiting for transfers between devices: 280 us -> 0 us
  Pallas kernels: 0 us -> 147 us
  matrix products: 100 us -> 0 us
  other arithmetic: 28.3 us -> 0 us
  local copies, waits for them, and re-layouts: 20.7 us -> 6.42 us
  between operations: 14.7 us -> 0.64 us
  starting transfers between devices: 7.05 us -> 0 us
    reduce_scatter x1 -> x0, waiting for transfers between devices: 151 us -> none  [body(): lax.psum_scatter(lax.dot_general(normed, grad_qkv, (((0,), (0,)), ((), ()...]
    pallas_call x0 -> x1, Pallas kernels: none -> 147 us  [body(): pl.pallas_call(kernel, out_shape=(jax.ShapeDtypeStruct((ROWS, D), BF16),...]
    dot_general x9 -> x0, matrix products: 81.5 us -> none  [the longest x1 18.6 us: body(): jnp.einsum('qhd,khd->hqk', grad_heads, value_heads, preferred_element_typ...]
    ppermute x2 -> x0, waiting for transfers between devices: 69.7 us -> none  [from_behind(): return lax.ppermute(array, axis, pairs)]
    psum x1 -> x0, waiting for transfers between devices: 59.1 us -> none  [body(): total = lax.psum(share, 'dp').astype(jnp.float32)]
    sub x1 -> x0, matrix products: 18.7 us -> none  [soft_probs(): expo = jnp.exp(scores - top)]
    convert_element_type x2 -> x0, other arithmetic: 16.6 us -> none  [the longest x1 13.1 us: body(): probs.astype(jnp.bfloat16)]
    concatenate x2 -> x0, local copies, waits for them, and re-layouts: 7.85 us -> none  [the longest x1 3.94 us: body(): values_ext = jnp.concatenate([before[:, width:], qkv[:, 2 * width:]], 0)]
  transfers between devices with their start and end apart: 4 -> 0, of which waited for: 4 -> 0; matrix products, arithmetic and copies ran while one was open for 7% -> 0% of each run, Pallas kernels for 0% -> 0%
where the time goes in v1:
time: 155 us; the launch traced here: 154 us
  Pallas kernels  147 us (95%)
  local copies, waits for them, and re-layouts  6.42 us (4%)
    pallas_call x1, Pallas kernels, body(): pl.pallas_call(kernel, out_shape=(jax.ShapeDtypeStruct((ROWS, D), BF16),...  147 us
    unnamed x2, local copies, waits for them, and re-layouts  4.03 us

profile of v1, /device:TPU:1, one launch (start us, length us, event | category | flops | bytes accessed | tf_op | source)
XLA Modules:
  0.0 154.3 jit_solution(6954139834284182186)
XLA Ops:
  0.6 0.8 pad_dynamic-slice_fusion
  1.4 0.6 slice.3
  2.0 1.0 copy.8.segk_ref
  3.0 147.2 %shard_map.77 = (bf16[512,1024]{1,0:T(8,128)(2,1)}, f32[32,3072]{1,0:T(8,128)}) custom-call(bf16[512,1024]{1,0:T(8,128)(2,1)} %bitcast.8, bf16[512,1024]{1,0:T(8,128)(2,1)} %bitcast.9, f32[1,1024]{1,0:T(1,128)} %bitcast.13, bf16[1024,3072]{1,0:T(8,128)(2,1)} %w_hbm.1, bf16[1024,1024]{1,0:T(8,128)(2,1)} %wo_hbm.1, s32[1,512]{1,0:T(1,128)} %bitcast.12, ...), custom_call_target="tpu_custom_call" | custom-call | tf_op jit(solution)/shard_map/pallas_call | solution.py:462
  150.3 2.3 %copy.11 = bf16[1,512,1024]{2,1,0:T(8,128)(2,1)} copy(bf16[1,512,1024]{2,1,0:T(8,128)(2,1)} %bitcast.7) | data formatting | bytes 2097152
  152.5 1.8 %copy.12 = f32[32,3072]{1,0:T(8,128)} copy(f32[32,3072]{1,0:T(8,128)} %get-tuple-element.9) | data formatting | bytes 786432

commit v2 on v1

--- a/solution.py
+++ b/solution.py
@@ -35,10 +35,11 @@
     ("zw", "yu", "zu", "yw", "xu", "xw"),
     ("yu", "zw", "yw", "zu", "xw", "xu"),
     ("zu", "yw", "zw", "yu", "xu", "xw"),
-    ("yw", "zw", "yu", "zu", "xw", "xu"),
-    ("zw", "yw", "zu", "yu", "xu", "xw"),
+    ("xw", "zu", "yw", "xu", "yu", "zw"),
+    ("xu", "yw", "zu", "xw", "zw", "yu"),
 )
 STEPS = len(ORDERS[0])
+SEQUENCE = (3, 0, 1, 2)
 BLOCK = 16
 BLOCKS = D // BLOCK
 
@@ -158,7 +159,7 @@
                 device_id_type=MESH,
             )
         )
-    for piece in reversed(range(NQ)):
+    for piece in SEQUENCE:
         halos[piece].start()
 
     gain = gain_ref[...]
@@ -250,57 +251,74 @@
             [dq_t[: PAIR // 2, :QB], dq_t[PAIR // 2 :, QB:]], 0
         )
         dq_ref[lo : lo + QB, at] = (dq_t.T * SCALE).astype(BF16)
-        fresh = SPAN if j == NQ - 1 else QB
-        done = SPAN if j == 0 else QB
-        for part, acc_ref, out_ref, scale in (
-            (part_v, accv_ref, dv_ref, 1.0),
-            (part_k, acck_ref, dk_ref, SCALE),
-        ):
-            for r in range(0, SPAN, QB):
+        for r in range(0, SPAN, QB):
+            block = (lo + r) // QB
+            reached = [i for i in SEQUENCE if i <= block <= i + SPAN // QB - 1]
+            rows = slice(lo + r, lo + r + QB)
+            for part, acc_ref, out_ref, scale in (
+                (part_v, accv_ref, dv_ref, 1.0),
+                (part_k, acck_ref, dk_ref, SCALE),
+            ):
                 value = part[r : r + QB]
-                if r >= fresh:
-                    value = acc_ref[lo + r : lo + r + QB, at] + value
-                if r >= SPAN - done:
-                    out_ref[lo + r : lo + r + QB, at] = (value * scale).astype(BF16)
+                if j != reached[0]:
+                    value = acc_ref[rows, at] + value
+                if j == reached[-1]:
+                    out_ref[rows, at] = (value * scale).astype(BF16)
                 else:
-                    acc_ref[lo + r : lo + r + QB, at] = value
-
-    for j in reversed(range(NQ)):
+                    acc_ref[rows, at] = value
+
+    def arrive(j):
         halos[j].wait_recv()
         normed = norm_rows(xh_ref, j * QB, j * QB)
         nt_ref[:, j * QB : (j + 1) * QB] = normed.T
         keys_values(j * QB, QB)
 
+    backs = {}
+
+    def give_back(b):
+        rows = slice(b * QB, (b + 1) * QB)
+
+        @pl.loop(0, D // TILE)
+        def _(n):
+            at = pl.ds(pl.multiple_of(n * TILE, TILE), TILE)
+            back_send[b, :, at] = (
+                lax.dot_general(
+                    dk_ref[rows, :], w_ref[at, D : 2 * D], NT, preferred_element_type=F32
+                )
+                + lax.dot_general(
+                    dv_ref[rows, :], w_ref[at, 2 * D :], NT, preferred_element_type=F32
+                )
+            ).astype(BF16)
+
+        backs[b] = pltpu.make_async_remote_copy(
+            src_ref=back_send.at[b],
+            dst_ref=back_recv.at[b],
+            send_sem=back_sem.at[0, b],
+            recv_sem=back_sem.at[1, b],
+            device_id=prev,
+            device_id_type=MESH,
+        )
+        backs[b].start()
+
+    arrived = set()
+    for step, j in enumerate(SEQUENCE):
+        for piece in SEQUENCE:
+            if piece >= j and piece not in arrived:
+                arrived.add(piece)
+                arrive(piece)
+
         @pl.loop(0, PAIRS // 2)
         def _(p):
             attend(j, p * 2)
             attend(j, p * 2 + 1)
 
-    backs = []
-    for n in range(D // TILE):
-        at = pl.ds(n * TILE, TILE)
-        back_send[n] = (
-            lax.dot_general(
-                dk_ref[:WINDOW, :], w_ref[at, D : 2 * D], NT, preferred_element_type=F32
-            )
-            + lax.dot_general(
-                dv_ref[:WINDOW, :], w_ref[at, 2 * D :], NT, preferred_element_type=F32
-            )
-        ).astype(BF16)
-        copy = pltpu.make_async_remote_copy(
-            src_ref=back_send.at[n],
-            dst_ref=back_recv.at[n],
-            send_sem=back_sem.at[0, n],
-            recv_sem=back_sem.at[1, n],
-            device_id=prev,
-            device_id_type=MESH,
-        )
-        copy.start()
-        backs.append(copy)
+        for b in range(NQ):
+            if all(i in SEQUENCE[: step + 1] for i in range(b + 1)) and b not in backs:
+                give_back(b)
 
     places = [block_places(order) for order in ORDERS]
 
-    def weight_half(c, half, out_ref):
+    def weight_half(c, half, out_ref, add_ref=None):
         part, lo = c // 2, c % 2 * 2 * HALF
         at = pl.ds(pl.multiple_of(lo + half * HALF, HALF), HALF)
         if part == 0:
@@ -310,13 +328,12 @@
         else:
             grads = dk_ref if part == 1 else dv_ref
             value = jnp.dot(nt_ref[...], grads[:, at], preferred_element_type=F32)
-        value = value.astype(BF16)
         for block, place in enumerate(places[c]):
-            out_ref[c, place * BLOCK : (place + 1) * BLOCK, :] = value[
-                block * BLOCK : (block + 1) * BLOCK
-            ]
-
-    sends = []
+            rows = slice(place * BLOCK, (place + 1) * BLOCK)
+            piece = value[block * BLOCK : (block + 1) * BLOCK]
+            if add_ref is not None:
+                piece = piece + add_ref[c, rows, :].astype(F32)
+            out_ref[c, rows, :] = piece.astype(BF16)
 
     def sibling_copy(c):
         return pltpu.make_async_remote_copy(
@@ -364,24 +381,12 @@
                 own_ref[c, to, :].astype(F32) + src_ref[c, frm, :].astype(F32)
             ).astype(BF16)
 
-    def stage(c, i):
-        if i == 0:
-            weight_half(c, 1 - core, sib_send)
-            sib_copies[c] = sibling_copy(c)
-            sib_copies[c].start()
-            weight_half(c, core, own_ref)
-        elif i == 1:
-            sib_copies[c].wait_recv()
-            add_rows(c, 0, sib_recv, 0, D)
-            halvings[c, 0] = halving_copy(c, 0)
-            halvings[c, 0].start()
-        else:
-            t = i - 2
-            halvings[c, t].wait_recv()
-            add_rows(c, base_of(c, t + 1), rs_recv, landing(t), D >> (t + 1))
-            if t + 1 < STEPS:
-                halvings[c, t + 1] = halving_copy(c, t + 1)
-                halvings[c, t + 1].start()
+    def stage(c, t):
+        halvings[c, t].wait_recv()
+        add_rows(c, base_of(c, t + 1), rs_recv, landing(t), D >> (t + 1))
+        if t + 1 < STEPS:
+            halvings[c, t + 1] = halving_copy(c, t + 1)
+            halvings[c, t + 1].start()
 
     def own_grad(n):
         at = pl.ds(n * TILE, TILE)
@@ -397,31 +402,33 @@
 
     def grad_rows(j):
         rows = slice(j * QB, (j + 1) * QB)
-        back = jnp.concatenate([back_recv[n, rows, :] for n in range(D // TILE)], 1)
         xf = x_ref[rows, :].astype(F32)
         inv = lax.rsqrt(jnp.mean(xf * xf, axis=1, keepdims=True) + EPS)
         normal = xf * inv
-        scaled = (gn_ref[rows, :] + back.astype(F32)) * gain
+        scaled = (gn_ref[rows, :] + back_recv[j].astype(F32)) * gain
         grad = (
             cot_ref[rows, :].astype(F32)
             + (scaled - normal * jnp.mean(scaled * normal, axis=1, keepdims=True)) * inv
         )
         gx_ref[rows, :] = grad.astype(BF16)
 
-    stages = STEPS + 2
-    for tick in range(CHUNKS + stages - 1):
+    for c in range(CHUNKS):
+        weight_half(c, 1 - core, sib_send)
+        sib_copies[c] = sibling_copy(c)
+        sib_copies[c].start()
+    for c in range(CHUNKS):
+        sib_copies[c].wait_recv()
+        weight_half(c, core, own_ref, sib_recv)
+        halvings[c, 0] = halving_copy(c, 0)
+        halvings[c, 0].start()
+    for n in range(D // TILE):
+        own_grad(n)
+    for t in range(STEPS):
         for c in range(CHUNKS):
-            if 0 <= tick - c < stages:
-                stage(c, tick - c)
-        if CHUNKS <= tick < CHUNKS + D // TILE:
-            own_grad(tick - CHUNKS)
-        if tick == CHUNKS + D // TILE:
-            for copy in backs:
-                copy.wait_recv()
-        if CHUNKS + D // TILE <= tick:
-            for j in (2 * (tick - CHUNKS - D // TILE), 2 * (tick - CHUNKS - D // TILE) + 1):
-                if j < NQ:
-                    grad_rows(j)
+            stage(c, t)
+        if t < NQ:
+            backs[t].wait_recv()
+            grad_rows(t)
 
     for c in range(CHUNKS):
         rows = pl.ds(pl.multiple_of(base_of(c, STEPS), BLOCK), BLOCK)
@@ -448,7 +455,7 @@
             at = pl.ds(pl.multiple_of(c * 2 * HALF + from_core * HALF, HALF), HALF)
             gw_ref[rows, at] = gather_ref[i, :, c * HALF : (c + 1) * HALF].astype(F32) * 0.25
 
-    for copy in (*halos, *backs, *sib_copies.values(), *halvings.values(), *copies):
+    for copy in (*halos, *backs.values(), *sib_copies.values(), *halvings.values(), *copies):
         copy.wait_send()
 
 
@@ -486,8 +493,8 @@
             pltpu.VMEM((EXT, D), BF16),
             pltpu.VMEM((EXT, D), F32),
             pltpu.VMEM((EXT, D), F32),
-            pltpu.VMEM((D // TILE, WINDOW, TILE), BF16),
-            pltpu.VMEM((D // TILE, WINDOW, TILE), BF16),
+            pltpu.VMEM((NQ, QB, D), BF16),
+            pltpu.VMEM((NQ, QB, D), BF16),
             pltpu.VMEM((ROWS, D), F32),
             pltpu.VMEM((CHUNKS, D, HALF), BF16),
             pltpu.VMEM((CHUNKS, D, HALF), BF16),
@@ -496,7 +503,7 @@
             pltpu.VMEM((4, BLOCK, CHUNKS * HALF), BF16),
             dma((4,)),
             dma((2, NQ)),
-            dma((2, D // TILE)),
+            dma((2, NQ)),
             dma((2, CHUNKS)),
             dma((CHUNKS, STEPS)),
             dma((CHUNKS, STEPS)),

time: 155 us -> 118 us (0.76)
  Pallas kernels: 147 us -> 110 us
    pallas_call x1, Pallas kernels: 147 us -> 110 us  [body(): pl.pallas_call(kernel, out_shape=(jax.ShapeDtypeStruct((ROWS, D), BF16),...]
where the time goes in v2:
time: 118 us
  Pallas kernels  110 us (93%)
  local copies, waits for them, and re-layouts  6.42 us (5%)
    pallas_call x1, Pallas kernels, body(): pl.pallas_call(kernel, out_shape=(jax.ShapeDtypeStruct((ROWS, D), BF16),...  110 us
    unnamed x2, local copies, waits for them, and re-layouts  4.03 us

profile of v2, /device:TPU:1, one launch (start us, length us, event | category | flops | bytes accessed | tf_op | source)
XLA Modules:
  0.0 117.5 jit_solution(5900539264506049093)
XLA Ops:
  0.6 0.8 pad_dynamic-slice_fusion
  1.4 0.6 slice.3
  2.0 1.0 copy.8.segk_ref
  3.0 110.5 %shard_map.77 = (bf16[512,1024]{1,0:T(8,128)(2,1)}, f32[32,3072]{1,0:T(8,128)}) custom-call(bf16[512,1024]{1,0:T(8,128)(2,1)} %bitcast.8, bf16[512,1024]{1,0:T(8,128)(2,1)} %bitcast.9, f32[1,1024]{1,0:T(1,128)} %bitcast.13, bf16[1024,3072]{1,0:T(8,128)(2,1)} %w_hbm.1, bf16[1024,1024]{1,0:T(8,128)(2,1)} %wo_hbm.1, s32[1,512]{1,0:T(1,128)} %bitcast.12, ...), custom_call_target="tpu_custom_call" | custom-call | tf_op jit(solution)/shard_map/pallas_call | solution.py:469
  113.5 2.3 %copy.11 = bf16[1,512,1024]{2,1,0:T(8,128)(2,1)} copy(bf16[1,512,1024]{2,1,0:T(8,128)(2,1)} %bitcast.7) | data formatting | bytes 2097152
  115.8 1.8 %copy.12 = f32[32,3072]{1,0:T(8,128)} copy(f32[32,3072]{1,0:T(8,128)} %get-tuple-element.9) | data formatting | bytes 786432

commit v3 on v2

--- a/solution.py
+++ b/solution.py
@@ -31,15 +31,16 @@
 NT = (((1,), (1,)), ((), ()))
 
 ORDERS = (
-    ("yw", "zu", "yu", "zw", "xw", "xu"),
-    ("zw", "yu", "zu", "yw", "xu", "xw"),
-    ("yu", "zw", "yw", "zu", "xw", "xu"),
-    ("zu", "yw", "zw", "yu", "xu", "xw"),
-    ("xw", "zu", "yw", "xu", "yu", "zw"),
-    ("xu", "yw", "zu", "xw", "zw", "yu"),
+    ("zw", "yw", "zu", "yu", "xw", "xu"),
+    ("zu", "yu", "zw", "yw", "xu", "xw"),
+    ("zw", "xw", "zu", "xu", "yw", "yu"),
+    ("zu", "xu", "zw", "xw", "yu", "yw"),
+    ("yw", "zw", "yu", "zu", "xw", "xu"),
+    ("yu", "zu", "yw", "zw", "xu", "xw"),
 )
 STEPS = len(ORDERS[0])
-SEQUENCE = (3, 0, 1, 2)
+SEQUENCE = (3, 2, 0, 1)
+RETURNS = {0: (0, 1), 1: (1, 3)}
 BLOCK = 16
 BLOCKS = D // BLOCK
 
@@ -88,11 +89,15 @@
     dv_ref,
     acck_ref,
     accv_ref,
+    expo_ref,
+    dprob_ref,
+    probs_a,
+    dscore_a,
+    probs_b,
+    dscore_b,
     back_send,
     back_recv,
-    gn_ref,
     own_ref,
-    sib_send,
     sib_recv,
     rs_recv,
     gather_ref,
@@ -159,7 +164,7 @@
                 device_id_type=MESH,
             )
         )
-    for piece in SEQUENCE:
+    for piece in reversed(range(NQ)):
         halos[piece].start()
 
     gain = gain_ref[...]
@@ -226,39 +231,47 @@
             [jnp.where(first_head, block, zero), jnp.where(first_head, zero, block)], 0
         )
 
-    def attend(j, pair):
+    def scores_of(j, pair, held):
+        at = pl.ds(pl.multiple_of(pair * PAIR, PAIR), PAIR)
+        span = slice(j * QB, j * QB + SPAN)
+        probs_ref, dscore_ref = held
+        state = {}
+
+        def scores():
+            queries = two_heads(q_ref[j * QB : (j + 1) * QB, at])
+            value = lax.dot_general(k_ref[span, at], queries, NT, preferred_element_type=F32)
+            mask = mask_ref[j]
+            value = value * (SCALE * LOG2E) + jnp.concatenate([mask, mask], 1)
+            expo_ref[...] = value
+            state["top"] = jnp.max(value, axis=0, keepdims=True)
+
+        def sums():
+            grads = two_heads(do_ref[j * QB : (j + 1) * QB, at])
+            expo = jnp.exp2(expo_ref[...] - state["top"])
+            dprob = lax.dot_general(v_ref[span, at], grads, NT, preferred_element_type=F32)
+            expo_ref[...] = expo
+            dprob_ref[...] = dprob
+            state["inverse"] = 1.0 / jnp.sum(expo, axis=0, keepdims=True)
+            total = jnp.sum(expo * dprob, axis=0, keepdims=True)
+            state["delta"] = total * state["inverse"]
+
+        def products():
+            probs = expo_ref[...] * state["inverse"]
+            probs_ref[...] = probs.astype(BF16)
+            dscore_ref[...] = (probs * (dprob_ref[...] - state["delta"])).astype(BF16)
+
+        return [scores, sums, products]
+
+    def grads_of(j, pair, held):
         at = pl.ds(pl.multiple_of(pair * PAIR, PAIR), PAIR)
         lo = j * QB
-        queries = two_heads(q_ref[lo : lo + QB, at])
-        grads = two_heads(do_ref[lo : lo + QB, at])
-        scores = lax.dot_general(
-            k_ref[lo : lo + SPAN, at], queries, NT, preferred_element_type=F32
-        )
-        dprob = lax.dot_general(
-            v_ref[lo : lo + SPAN, at], grads, NT, preferred_element_type=F32
-        )
-        mask = mask_ref[j]
-        scores = scores * (SCALE * LOG2E) + jnp.concatenate([mask, mask], 1)
-        expo = jnp.exp2(scores - jnp.max(scores, axis=0, keepdims=True))
-        inverse = 1.0 / jnp.sum(expo, axis=0, keepdims=True)
-        probs = expo * inverse
-        delta = jnp.sum(probs * dprob, axis=0, keepdims=True)
-        dscore = (probs * (dprob - delta)).astype(BF16)
-        part_v = jnp.dot(probs.astype(BF16), grads, preferred_element_type=F32)
-        part_k = jnp.dot(dscore, queries, preferred_element_type=F32)
-        dq_t = jnp.dot(kt_ref[at, lo : lo + SPAN], dscore, preferred_element_type=F32)
-        dq_t = jnp.concatenate(
-            [dq_t[: PAIR // 2, :QB], dq_t[PAIR // 2 :, QB:]], 0
-        )
-        dq_ref[lo : lo + QB, at] = (dq_t.T * SCALE).astype(BF16)
-        for r in range(0, SPAN, QB):
-            block = (lo + r) // QB
-            reached = [i for i in SEQUENCE if i <= block <= i + SPAN // QB - 1]
-            rows = slice(lo + r, lo + r + QB)
-            for part, acc_ref, out_ref, scale in (
-                (part_v, accv_ref, dv_ref, 1.0),
-                (part_k, acck_ref, dk_ref, SCALE),
-            ):
+        probs_ref, dscore_ref = held
+
+        def add_up(part, acc_ref, out_ref, scale):
+            for r in range(0, SPAN, QB):
+                block = (lo + r) // QB
+                reached = [i for i in SEQUENCE if i <= block <= i + SPAN // QB - 1]
+                rows = slice(lo + r, lo + r + QB)
                 value = part[r : r + QB]
                 if j != reached[0]:
                     value = acc_ref[rows, at] + value
@@ -267,6 +280,31 @@
                 else:
                     acc_ref[rows, at] = value
 
+        def values():
+            grads = two_heads(do_ref[lo : lo + QB, at])
+            part = jnp.dot(probs_ref[...], grads, preferred_element_type=F32)
+            add_up(part, accv_ref, dv_ref, 1.0)
+
+        def keys():
+            queries = two_heads(q_ref[lo : lo + QB, at])
+            part = jnp.dot(dscore_ref[...], queries, preferred_element_type=F32)
+            add_up(part, acck_ref, dk_ref, SCALE)
+
+        def queries():
+            part = jnp.dot(
+                kt_ref[at, lo : lo + SPAN], dscore_ref[...], preferred_element_type=F32
+            )
+            part = jnp.concatenate([part[: PAIR // 2, :QB], part[PAIR // 2 :, QB:]], 0)
+            dq_ref[lo : lo + QB, at] = (part.T * SCALE).astype(BF16)
+
+        return [values, keys, queries]
+
+    def side_by_side(one, other):
+        for i in range(3):
+            for steps in (one, other):
+                if steps:
+                    steps[i]()
+
     def arrive(j):
         halos[j].wait_recv()
         normed = norm_rows(xh_ref, j * QB, j * QB)
@@ -275,13 +313,13 @@
 
     backs = {}
 
-    def give_back(b):
-        rows = slice(b * QB, (b + 1) * QB)
+    def give_back(first, count):
+        rows = slice(first * QB, (first + count) * QB)
 
         @pl.loop(0, D // TILE)
         def _(n):
             at = pl.ds(pl.multiple_of(n * TILE, TILE), TILE)
-            back_send[b, :, at] = (
+            value = (
                 lax.dot_general(
                     dk_ref[rows, :], w_ref[at, D : 2 * D], NT, preferred_element_type=F32
                 )
@@ -289,34 +327,46 @@
                     dv_ref[rows, :], w_ref[at, 2 * D :], NT, preferred_element_type=F32
                 )
             ).astype(BF16)
-
-        backs[b] = pltpu.make_async_remote_copy(
-            src_ref=back_send.at[b],
-            dst_ref=back_recv.at[b],
-            send_sem=back_sem.at[0, b],
-            recv_sem=back_sem.at[1, b],
-            device_id=prev,
-            device_id_type=MESH,
-        )
-        backs[b].start()
-
+            for i in range(count):
+                back_send[first + i, :, at] = value[i * QB : (i + 1) * QB]
+
+        for b in range(first, first + count):
+            backs[b] = pltpu.make_async_remote_copy(
+                src_ref=back_send.at[b],
+                dst_ref=back_recv.at[b],
+                send_sem=back_sem.at[0, b],
+                recv_sem=back_sem.at[1, b],
+                device_id=prev,
+                device_id_type=MESH,
+            )
+            backs[b].start()
+
+    even, odd = (probs_a, dscore_a), (probs_b, dscore_b)
+    last = None
     arrived = set()
-    for step, j in enumerate(SEQUENCE):
-        for piece in SEQUENCE:
-            if piece >= j and piece not in arrived:
+    for j in SEQUENCE:
+        for piece in reversed(range(j, NQ)):
+            if piece not in arrived:
                 arrived.add(piece)
                 arrive(piece)
-
-        @pl.loop(0, PAIRS // 2)
+        side_by_side(scores_of(j, 0, even), last and grads_of(*last))
+        if last and last[0] in RETURNS:
+            give_back(*RETURNS[last[0]])
+        side_by_side(scores_of(j, 1, odd), grads_of(j, 0, even))
+
+        @pl.loop(1, PAIRS // 2)
         def _(p):
-            attend(j, p * 2)
-            attend(j, p * 2 + 1)
-
-        for b in range(NQ):
-            if all(i in SEQUENCE[: step + 1] for i in range(b + 1)) and b not in backs:
-                give_back(b)
+            side_by_side(scores_of(j, p * 2, even), grads_of(j, p * 2 - 1, odd))
+            side_by_side(scores_of(j, p * 2 + 1, odd), grads_of(j, p * 2, even))
+
+        last = (j, PAIRS - 1, odd)
+    side_by_side(None, grads_of(*last))
+    give_back(*RETURNS[last[0]])
 
     places = [block_places(order) for order in ORDERS]
+    sib_send = [
+        ref.at[:, i * HALF : (i + 1) * HALF] for ref in (k_ref, v_ref) for i in range(D // HALF)
+    ]
 
     def weight_half(c, half, out_ref, add_ref=None):
         part, lo = c // 2, c % 2 * 2 * HALF
@@ -332,12 +382,12 @@
             rows = slice(place * BLOCK, (place + 1) * BLOCK)
             piece = value[block * BLOCK : (block + 1) * BLOCK]
             if add_ref is not None:
-                piece = piece + add_ref[c, rows, :].astype(F32)
-            out_ref[c, rows, :] = piece.astype(BF16)
+                piece = piece + add_ref[rows, :].astype(F32)
+            out_ref[rows, :] = piece.astype(BF16)
 
     def sibling_copy(c):
         return pltpu.make_async_remote_copy(
-            src_ref=sib_send.at[c],
+            src_ref=sib_send[c],
             dst_ref=sib_recv.at[c],
             send_sem=sib_sem.at[0, c],
             recv_sem=sib_sem.at[1, c],
@@ -388,6 +438,8 @@
             halvings[c, t + 1] = halving_copy(c, t + 1)
             halvings[c, t + 1].start()
 
+    gn_ref = acck_ref.at[:ROWS]
+
     def own_grad(n):
         at = pl.ds(n * TILE, TILE)
         gn_ref[:, n * TILE : (n + 1) * TILE] = (
@@ -413,12 +465,12 @@
         gx_ref[rows, :] = grad.astype(BF16)
 
     for c in range(CHUNKS):
-        weight_half(c, 1 - core, sib_send)
+        weight_half(c, 1 - core, sib_send[c])
         sib_copies[c] = sibling_copy(c)
         sib_copies[c].start()
     for c in range(CHUNKS):
         sib_copies[c].wait_recv()
-        weight_half(c, core, own_ref, sib_recv)
+        weight_half(c, core, own_ref.at[c], sib_recv.at[c])
         halvings[c, 0] = halving_copy(c, 0)
         halvings[c, 0].start()
     for n in range(D // TILE):
@@ -426,9 +478,10 @@
     for t in range(STEPS):
         for c in range(CHUNKS):
             stage(c, t)
-        if t < NQ:
-            backs[t].wait_recv()
-            grad_rows(t)
+        if t == 1:
+            for j in range(2):
+                backs[j].wait_recv()
+                grad_rows(j)
 
     for c in range(CHUNKS):
         rows = pl.ds(pl.multiple_of(base_of(c, STEPS), BLOCK), BLOCK)
@@ -445,6 +498,9 @@
         )
         copy.start()
         copies.append(copy)
+    for j in range(2, NQ):
+        backs[j].wait_recv()
+        grad_rows(j)
     for i in range(4):
         if i:
             copies[i - 1].wait_recv()
@@ -493,10 +549,14 @@
             pltpu.VMEM((EXT, D), BF16),
             pltpu.VMEM((EXT, D), F32),
             pltpu.VMEM((EXT, D), F32),
+            pltpu.VMEM((SPAN, 2 * QB), F32),
+            pltpu.VMEM((SPAN, 2 * QB), F32),
+            pltpu.VMEM((SPAN, 2 * QB), BF16),
+            pltpu.VMEM((SPAN, 2 * QB), BF16),
+            pltpu.VMEM((SPAN, 2 * QB), BF16),
+            pltpu.VMEM((SPAN, 2 * QB), BF16),
             pltpu.VMEM((NQ, QB, D), BF16),
             pltpu.VMEM((NQ, QB, D), BF16),
-            pltpu.VMEM((ROWS, D), F32),
-            pltpu.VMEM((CHUNKS, D, HALF), BF16),
             pltpu.VMEM((CHUNKS, D, HALF), BF16),
             pltpu.VMEM((CHUNKS, D, HALF), BF16),
             pltpu.VMEM((CHUNKS, D, HALF), BF16),

time: 118 us -> 117 us (level)
    pallas_call x1, Pallas kernels: 110 us -> 109 us  [body(): pl.pallas_call(kernel, out_shape=(jax.ShapeDtypeStruct((ROWS, D), BF16),...]
where the time goes in v3:
time: 117 us; the launch traced here: 116 us
  Pallas kernels  109 us (93%)
  local copies, waits for them, and re-layouts  6.42 us (5%)
    pallas_call x1, Pallas kernels, body(): pl.pallas_call(kernel, out_shape=(jax.ShapeDtypeStruct((ROWS, D), BF16),...  109 us
    unnamed x2, local copies, waits for them, and re-layouts  4.03 us

profile of v3, /device:TPU:1, one launch (start us, length us, event | category | flops | bytes accessed | tf_op | source)
XLA Modules:
  0.0 116.3 jit_solution(1501934288277254293)
XLA Ops:
  0.6 0.8 pad_dynamic-slice_fusion
  1.4 0.6 slice.3
  2.0 1.0 copy.8.segk_ref
  3.0 109.2 %shard_map.77 = (bf16[512,1024]{1,0:T(8,128)(2,1)}, f32[32,3072]{1,0:T(8,128)}) custom-call(bf16[512,1024]{1,0:T(8,128)(2,1)} %bitcast.8, bf16[512,1024]{1,0:T(8,128)(2,1)} %bitcast.9, f32[1,1024]{1,0:T(1,128)} %bitcast.13, bf16[1024,3072]{1,0:T(8,128)(2,1)} %w_hbm.1, bf16[1024,1024]{1,0:T(8,128)(2,1)} %wo_hbm.1, s32[1,512]{1,0:T(1,128)} %bitcast.12, ...), custom_call_target="tpu_custom_call" | custom-call | tf_op jit(solution)/shard_map/pallas_call | solution.py:525
  112.3 2.3 %copy.11 = bf16[1,512,1024]{2,1,0:T(8,128)(2,1)} copy(bf16[1,512,1024]{2,1,0:T(8,128)(2,1)} %bitcast.7) | data formatting | bytes 2097152
  114.5 1.8 %copy.12 = f32[32,3072]{1,0:T(8,128)} copy(f32[32,3072]{1,0:T(8,128)} %get-tuple-element.9) | data formatting | bytes 786432

commit v4 on v3

--- a/solution.py
+++ b/solution.py
@@ -31,12 +31,12 @@
 NT = (((1,), (1,)), ((), ()))
 
 ORDERS = (
-    ("zw", "yw", "zu", "yu", "xw", "xu"),
+    ("yw", "zu", "yu", "zw", "xw", "xu"),
+    ("zw", "yu", "zu", "yw", "xu", "xw"),
+    ("yu", "zw", "yw", "zu", "xw", "xu"),
+    ("zu", "yw", "zw", "yu", "xu", "xw"),
+    ("yw", "zw", "yu", "zu", "xw", "xu"),
     ("zu", "yu", "zw", "yw", "xu", "xw"),
-    ("zw", "xw", "zu", "xu", "yw", "yu"),
-    ("zu", "xu", "zw", "xw", "yu", "yw"),
-    ("yw", "zw", "yu", "zu", "xw", "xu"),
-    ("yu", "zu", "yw", "zw", "xu", "xw"),
 )
 STEPS = len(ORDERS[0])
 SEQUENCE = (3, 2, 0, 1)
@@ -509,7 +509,7 @@
         rows = pl.ds(pl.multiple_of(from_zh * BLOCK, BLOCK), BLOCK)
         for c in range(CHUNKS):
             at = pl.ds(pl.multiple_of(c * 2 * HALF + from_core * HALF, HALF), HALF)
-            gw_ref[rows, at] = gather_ref[i, :, c * HALF : (c + 1) * HALF].astype(F32) * 0.25
+            gw_ref[rows, at] = gather_ref[i, :, c * HALF : (c + 1) * HALF]
 
     for copy in (*halos, *backs.values(), *sib_copies.values(), *halvings.values(), *copies):
         copy.wait_send()
@@ -526,7 +526,7 @@
         kernel,
         out_shape=(
             jax.ShapeDtypeStruct((ROWS, D), BF16),
-            jax.ShapeDtypeStruct((2 * BLOCK, 3 * D), F32),
+            jax.ShapeDtypeStruct((2 * BLOCK, 3 * D), BF16),
         ),
         in_specs=[any_space, any_space, vmem, any_space, any_space, vmem, vmem],
         out_specs=(vmem, vmem),
@@ -581,7 +581,7 @@
         seg[None, WINDOW:],
         seg[:, None],
     )
-    return grad_x[None], grad_w
+    return grad_x[None], grad_w.astype(F32) * (1 / 4)
 
 
 def solution(mesh):

time: 117 us -> 113 us (0.966)
  Pallas kernels: 109 us -> 104 us
  local copies, waits for them, and re-layouts: 6.42 us -> 4.65 us
  other arithmetic: 0 us -> 1.7 us
    pallas_call x1, Pallas kernels: 109 us -> 104 us  [body(): pl.pallas_call(kernel, out_shape=(jax.ShapeDtypeStruct((ROWS, D), BF16),...]
    unnamed x2 -> x1, local copies, waits for them, and re-layouts: 4.03 us -> 2.26 us
    mul x0 -> x1, other arithmetic: none -> 1.7 us  [body(): return (grad_x[None], grad_w.astype(F32) * (1 / 4))]
where the time goes in v4:
time: 113 us; the launch traced here: 111 us
  Pallas kernels  104 us (92%)
  local copies, waits for them, and re-layouts  4.65 us (4%)
  other arithmetic  1.7 us (2%)
    pallas_call x1, Pallas kernels, body(): pl.pallas_call(kernel, out_shape=(jax.ShapeDtypeStruct((ROWS, D), BF16),...  104 us
    unnamed x1, local copies, waits for them, and re-layouts  2.26 us

profile of v4, /device:TPU:1, one launch (start us, length us, event | category | flops | bytes accessed | tf_op | source)
XLA Modules:
  0.0 111.4 jit_solution(16817225236965591424)
XLA Ops:
  0.6 0.8 pad_dynamic-slice_fusion
  1.4 0.6 slice.3
  2.0 1.0 copy.8.segk_ref
  3.0 104.4 %shard_map.77 = (bf16[512,1024]{1,0:T(8,128)(2,1)}, bf16[32,3072]{1,0:T(8,128)(2,1)}) custom-call(bf16[512,1024]{1,0:T(8,128)(2,1)} %bitcast.8, bf16[512,1024]{1,0:T(8,128)(2,1)} %bitcast.9, f32[1,1024]{1,0:T(1,128)} %bitcast.13, bf16[1024,3072]{1,0:T(8,128)(2,1)} %w_hbm.1, bf16[1024,1024]{1,0:T(8,128)(2,1)} %wo_hbm.1, s32[1,512]{1,0:T(1,128)} %bitcast.12, ...), custom_call_target="tpu_custom_call" | custom-call | tf_op jit(solution)/shard_map/pallas_call | solution.py:525
  107.5 1.7 %convert_multiply_fusion = f32[32,3072]{1,0:T(8,128)} fusion(bf16[32,3072]{1,0:T(8,128)(2,1)} %get-tuple-element.5), kind=kLoop, calls=%fused_computation | loop fusion | flops 196608 | bytes 589824 | tf_op jit(solution)/shard_map/mul | solution.py:584
  109.2 2.3 %copy.10 = bf16[1,512,1024]{2,1,0:T(8,128)(2,1)} copy(bf16[1,512,1024]{2,1,0:T(8,128)(2,1)} %bitcast.7) | data formatting | bytes 2097152

commit v5 on v4

--- a/solution.py
+++ b/solution.py
@@ -67,8 +67,7 @@
     gain_ref,
     w_hbm,
     wo_hbm,
-    segq_ref,
-    segk_ref,
+    seg_ref,
     gx_ref,
     gw_ref,
     x_ref,
@@ -185,8 +184,11 @@
     lane = lax.broadcasted_iota(jnp.int32, (SPAN, QB), 1)
     row = lax.broadcasted_iota(jnp.int32, (SPAN, QB), 0)
     in_window = (row > lane) & (row <= lane + WINDOW)
+    seg = seg_ref[...].astype(F32)
+    seg_keys = jnp.broadcast_to(seg, (QB, EXT)).T
     for j in range(NQ):
-        same = segk_ref[j * QB : j * QB + SPAN, :] == segq_ref[:, j * QB : (j + 1) * QB]
+        seg_queries = seg[:, WINDOW + j * QB : WINDOW + (j + 1) * QB]
+        same = seg_keys[j * QB : j * QB + SPAN, :] == seg_queries
         mask_ref[j] = jnp.where(in_window & same, 0.0, -1e30).astype(F32)
 
     loads[1].wait()
@@ -528,7 +530,7 @@
             jax.ShapeDtypeStruct((ROWS, D), BF16),
             jax.ShapeDtypeStruct((2 * BLOCK, 3 * D), BF16),
         ),
-        in_specs=[any_space, any_space, vmem, any_space, any_space, vmem, vmem],
+        in_specs=[any_space, any_space, vmem, any_space, any_space, vmem],
         out_specs=(vmem, vmem),
         scratch_shapes=[
             pltpu.VMEM((ROWS, D), BF16),
@@ -578,8 +580,7 @@
         gain[None],
         w_qkv,
         w_out,
-        seg[None, WINDOW:],
-        seg[:, None],
+        seg[None],
     )
     return grad_x[None], grad_w.astype(F32) * (1 / 4)
 

time: 113 us -> 111 us (0.982)
  no operation moved by 1% of the time
where the time goes in v5:
time: 111 us; the launch traced here: 110 us
  Pallas kernels  104 us (94%)
  local copies, waits for them, and re-layouts  3.63 us (3%)
  other arithmetic  1.7 us (2%)
    pallas_call x1, Pallas kernels, body(): pl.pallas_call(kernel, out_shape=(jax.ShapeDtypeStruct((ROWS, D), BF16),...  104 us
    unnamed x1, local copies, waits for them, and re-layouts  2.26 us

profile of v5, /device:TPU:1, one launch (start us, length us, event | category | flops | bytes accessed | tf_op | source)
XLA Modules:
  0.0 109.9 jit_solution(1104733582251128989)
XLA Ops:
  0.6 1.4 %pad_dynamic-slice_fusion = s32[1024]{0:T(1024)} fusion(s32[]{:T(128)S(6)} %select_n.3, s32[16384]{0:T(1024)} %bitcast.9), kind=kLoop, calls=%fused_computation.1 | loop fusion | bytes 69636 | tf_op jit(solution)/shard_map/dynamic_slice | solution.py:523
  2.0 104.0 %shard_map.77 = (bf16[512,1024]{1,0:T(8,128)(2,1)}, bf16[32,3072]{1,0:T(8,128)(2,1)}) custom-call(bf16[512,1024]{1,0:T(8,128)(2,1)} %bitcast.6, bf16[512,1024]{1,0:T(8,128)(2,1)} %bitcast.7, f32[1,1024]{1,0:T(1,128)} %bitcast.11, bf16[1024,3072]{1,0:T(8,128)(2,1)} %w_hbm.1, bf16[1024,1024]{1,0:T(8,128)(2,1)} %wo_hbm.1, s32[1,1024]{1,0:T(1,128)} %bitcast.10), custom_call_target="tpu_custom_call" | custom-call | tf_op jit(solution)/shard_map/pallas_call | solution.py:527
  106.0 1.7 %convert_multiply_fusion = f32[32,3072]{1,0:T(8,128)} fusion(bf16[32,3072]{1,0:T(8,128)(2,1)} %get-tuple-element.5), kind=kLoop, calls=%fused_computation | loop fusion | flops 196608 | bytes 589824 | tf_op jit(solution)/shard_map/mul | solution.py:585
  107.7 2.3 %copy.9 = bf16[1,512,1024]{2,1,0:T(8,128)(2,1)} copy(bf16[1,512,1024]{2,1,0:T(8,128)(2,1)} %bitcast.8) | data formatting | bytes 2097152
